TPU v7x, 32 devices: a whole 2x2x4 slice. The times are simulated.
32 devices in a mesh: groups: 2 (over y), row: 4 (over x, core), col: 4 (over z).
Axes of the slice: x: 2, y: 2, z: 4, core: 2. Of those that a mesh axis runs over, the one named last changes fastest.
Arguments:
- features: float32 [32, 65536], P(None, ('groups', 'row', 'col')), parts along dimension 1, may hold values from -6 to 6
- noise: float32 [65536], P(('groups', 'row', 'col')), parts along dimension 0, may hold values from 0.5 to 4
- solution: float32 [16, 65536], P(None, ('groups', 'row', 'col')), parts along dimension 1, may hold values from -6 to 6
- residual: float32 [16, 65536], P(None, ('groups', 'row', 'col')), parts along dimension 1, may hold values from -12 to 12
- direction: float32 [16, 65536], P(None, ('groups', 'row', 'col')), parts along dimension 1, may hold values from -12 to 12
- tile_rows: int32 [8, 4, 64], P(('groups', 'row'), 'col'), parts along dimension 0, may hold values from 0 to 15, as said below
- tile_cols: int32 [8, 4, 64], P(('groups', 'row'), 'col'), parts along dimension 0, may hold values from 0 to 15, as said below
- tile_count: int32 [8, 4], P(('groups', 'row'), 'col'), parts along dimension 0, may hold values from 1 to 64, as said below
Outputs:
- solution_next: float32 [16, 65536], P(None, ('groups', 'row', 'col')), parts along dimension 1
- residual_next: float32 [16, 65536], P(None, ('groups', 'row', 'col')), parts along dimension 1
- direction_next: float32 [16, 65536], P(None, ('groups', 'row', 'col')), parts along dimension 1
There are 2 independent parts, one for each index of `groups`. A program takes and returns all parts, laid end to end along the dimension named above; each array names one. Nothing has to cross between parts.
Inputs may be any that keep to these rules, and one draw needn't show every extreme that they name: `tile_rows`: every listed slot names a tile with I <= J; the slots of one device name distinct tiles. `tile_cols`: see tile_rows. `tile_count`: some device of every problem lists 64 tiles.
All inputs are finite; a program needn't handle non-finite values.
Results may differ from a plain program's by a relative error of at most 0.0003.
Values sent between devices are 32-bit elements; how exact they have to be, the bound alone decides.
A program may use at most 64 MiB of HBM per device.

v0:
```python
import math
import jax
import jax.numpy as jnp
from jax import lax
from jax.sharding import PartitionSpec as P

BLK_DEV = 4
HIGH = lax.Precision.HIGHEST


def tile_kernel(row_points, col_points):
    inner = lax.dot_general(
        row_points,
        col_points,
        (((0,), (0,)), ((), ())),
        precision=HIGH,
        preferred_element_type=jnp.float32,
    )
    row_norms = jnp.sum(row_points * row_points, 0)
    col_norms = jnp.sum(col_points * col_points, 0)
    dist_sq = jnp.maximum(row_norms[:, None] + col_norms[None, :] - 2.0 * inner, 0.0)
    radius = jnp.sqrt(dist_sq) / (1.5 * math.sqrt(row_points.shape[0]))
    inside = jnp.maximum(1.0 - radius, 0.0)
    return inside**4 * (4.0 * radius + 1.0)


def gram(left, right):
    return lax.dot_general(
        left, right, (((1,), (1,)), ((), ())), precision=HIGH, preferred_element_type=jnp.float32
    )


def symmetric(matrix):
    return 0.5 * (matrix + matrix.T)


def spd_solve(matrix, target):
    lower = jnp.linalg.cholesky(matrix)
    half_way = lax.linalg.triangular_solve(lower, target, left_side=True, lower=True)
    return lax.linalg.triangular_solve(
        lower, half_way, left_side=True, lower=True, transpose_a=True
    )


def apply_left(coeffs, field):
    return lax.dot_general(
        coeffs, field, (((0,), (0,)), ((), ())), precision=HIGH, preferred_element_type=jnp.float32
    )


def add_at(running, addend, start):
    axis_last = running.ndim - 1
    current = lax.dynamic_slice_in_dim(running, start, addend.shape[-1], axis_last)
    return lax.dynamic_update_slice_in_dim(running, current + addend, start, axis_last)


def reduce_rows(row_image, row_degree):
    return (
        lax.psum_scatter(row_image, "col", scatter_dimension=1, tiled=True),
        lax.psum_scatter(row_degree, "col", scatter_dimension=0, tiled=True),
    )


def reduce_cols(col_image, col_degree):
    return (
        lax.psum_scatter(col_image, "row", scatter_dimension=1, tiled=True),
        lax.psum_scatter(col_degree, "row", scatter_dimension=0, tiled=True),
    )


def on_device(features, noise, solution, residual, direction, tile_rows, tile_cols, tile_count):
    block_width = features.shape[1] // BLK_DEV
    row_slots = tile_rows[0, 0]
    col_slots = tile_cols[0, 0]
    tile_total = tile_count[0, 0]
    rank_row = lax.axis_index("row")
    rank_col = lax.axis_index("col")
    span = lax.axis_size("col") * BLK_DEV
    row_feat, row_dir = (
        lax.all_gather(features, "col", axis=1, tiled=True),
        lax.all_gather(direction, "col", axis=1, tiled=True),
    )
    col_feat, col_dir = (
        lax.all_gather(features, "row", axis=1, tiled=True),
        lax.all_gather(direction, "row", axis=1, tiled=True),
    )
    side_count = direction.shape[0]
    initial = (
        jnp.zeros((side_count, row_feat.shape[1]), jnp.float32),
        jnp.zeros((row_feat.shape[1],), jnp.float32),
        jnp.zeros((side_count, col_feat.shape[1]), jnp.float32),
        jnp.zeros((col_feat.shape[1],), jnp.float32),
    )

    def one_tile(tile_slot, carried):
        to_row, deg_row, to_col, deg_col = carried
        local_i = row_slots[tile_slot]
        local_j = col_slots[tile_slot]
        start_i = local_i * block_width
        start_j = local_j * block_width
        used_flag = (tile_slot < tile_total).astype(jnp.float32)
        kernel = (
            tile_kernel(
                lax.dynamic_slice_in_dim(row_feat, start_i, block_width, 1),
                lax.dynamic_slice_in_dim(col_feat, start_j, block_width, 1),
            )
            * used_flag
        )
        dir_cols = lax.dynamic_slice_in_dim(col_dir, start_j, block_width, 1)
        row_term = lax.dot_general(
            dir_cols,
            kernel,
            (((1,), (1,)), ((), ())),
            precision=HIGH,
            preferred_element_type=jnp.float32,
        )
        to_row = add_at(to_row, row_term, start_i)
        deg_row = add_at(deg_row, jnp.sum(kernel, 1), start_i)
        big_i = rank_row * span + local_i
        big_j = local_j // BLK_DEV * span + rank_col * BLK_DEV + local_j % BLK_DEV
        mirror = (big_i != big_j).astype(jnp.float32)
        dir_rows = lax.dynamic_slice_in_dim(row_dir, start_i, block_width, 1)
        col_term = (
            lax.dot_general(
                dir_rows,
                kernel,
                (((1,), (0,)), ((), ())),
                precision=HIGH,
                preferred_element_type=jnp.float32,
            )
            * mirror
        )
        to_col = add_at(to_col, col_term, start_j)
        deg_col = add_at(deg_col, jnp.sum(kernel, 0) * mirror, start_j)
        return (to_row, deg_row, to_col, deg_col)

    def one_turn(turn_index, carried):
        for inner_step in range(4):
            carried = one_tile(turn_index * 4 + inner_step, carried)
        return carried

    carried = lax.fori_loop(0, row_slots.shape[0] // 4, one_turn, initial)
    row_image, row_degree = reduce_rows(carried[0], carried[1])
    col_image, col_degree = reduce_cols(carried[2], carried[3])
    degree = row_degree + col_degree
    image = (noise + degree)[None, :] * direction + row_image + col_image
    curv_sum, norm_sum = lax.psum(
        (gram(direction, image), gram(residual, residual)), ("row", "col")
    )
    curvature = symmetric(curv_sum)
    norms_now = symmetric(norm_sum)
    alpha = spd_solve(curvature, norms_now)
    residual_next = residual - apply_left(alpha, image)
    norms_next = symmetric(lax.psum(gram(residual_next, residual_next), ("row", "col")))
    solution_next = solution + apply_left(alpha, direction)
    beta = spd_solve(norms_now, norms_next)
    direction_next = residual_next + apply_left(beta, direction)
    return (solution_next, residual_next, direction_next)


def solution(mesh):
    in_specs = (
        P(None, ("groups", "row", "col")),
        P(("groups", "row", "col")),
        P(None, ("groups", "row", "col")),
        P(None, ("groups", "row", "col")),
        P(None, ("groups", "row", "col")),
        P(("groups", "row"), "col", None),
        P(("groups", "row"), "col", None),
        P(("groups", "row"), "col"),
    )
    out_specs = (
        P(None, ("groups", "row", "col")),
        P(None, ("groups", "row", "col")),
        P(None, ("groups", "row", "col")),
    )
    return jax.shard_map(
        on_device, mesh=mesh, in_specs=in_specs, out_specs=out_specs, check_vma=False
    )
```

profile of v0, /device:TPU:0, one launch (start us, length us, event | category | flops | bytes accessed | tf_op | source)
XLA Modules:
  0.0 874.8 jit_solution(3112990234694962577)
XLA Ops:
  8.8 20.4 %all_gather.15 = f32[16,8192]{1,0:T(8,128)S(1)} all-gather(f32[16,2048]{1,0:T(8,128)S(1)} %copy-done), channel_id=1, replica_groups=mesh['groups'=2,'row'=4,'col'=4] {'col'}, dimensions={1}, use_global_device_ids=true | all-gather | bytes 655360 | tf_op jit(solution)/shard_map/all_gather | solution.py:81
  29.2 7.2 all_gather.12
  36.4 6.0 all-gather.3.cloned.1.call-done
  42.4 17.7 %all-gather.5.cloned.1.call-done = f32[32,8192]{1,0:T(8,128)} async-done(((f32[32,2048]{1,0:T(8,128)}), f32[32,8192]{1,0:T(8,128)}) %all-gather.5.cloned.1.call-update) | async-done | bytes 1048592 | tf_op jit(solution)/shard_map/all_gather | solution.py:84
  60.9 658.1 %while.22 = (s32[]{:T(128)}, f32[16,8192]{1,0:T(8,128)S(1)}, f32[8192]{0:T(1024)S(1)}, f32[16,8192]{1,0:T(8,128)S(1)}, f32[8192]{0:T(1024)S(1)}, /*index=5*/s32[...) while((s32[]{:T(128)}, f32[16,8192]{1,0:T(8,128)S(1)}, ...), condition=%wide.region_17.18_spmd, body=%wide.region_0.17_spmd.sunk | while | flops 821393472 | bytes 14518369 | solution.py:142
  83.6 2.7 fusion.148
  88.2 2.7 fusion.150
  92.8 2.7 fusion.152
  124.8 2.7 fusion.148
  129.4 2.7 fusion.150
  134.0 2.7 fusion.152
  165.9 2.7 fusion.148
  170.5 2.7 fusion.150
  207.0 2.7 fusion.148
  211.6 2.7 fusion.150
  216.2 2.7 fusion.152
  248.2 2.7 fusion.148
  252.8 2.7 fusion.150
  289.3 2.7 fusion.148
  293.9 2.7 fusion.150
  330.4 2.7 fusion.148
  335.0 2.7 fusion.150
  371.5 2.7 fusion.148
  376.2 2.7 fusion.150
  380.7 2.7 fusion.152
  412.7 2.7 fusion.148
  417.3 2.7 fusion.150
  453.8 2.7 fusion.148
  458.4 2.7 fusion.150
  494.9 2.7 fusion.148
  499.5 2.7 fusion.150
  536.1 2.7 fusion.148
  540.7 2.7 fusion.150
  577.2 2.7 fusion.148
  581.8 2.7 fusion.150
  618.3 2.7 fusion.148
  622.9 2.7 fusion.150
  659.4 2.7 fusion.148
  664.0 2.7 fusion.150
  700.5 2.7 fusion.148
  705.1 2.7 fusion.150
  709.7 2.7 fusion.152
  714.3 2.7 fusion.154
  723.8 10.9 %all-reduce.1 = f32[8192]{0:T(1024)S(1)} all-reduce(f32[8192]{0:T(1024)S(1)} %get-tuple-element.410), channel_id=3, replica_groups=mesh['groups'=2,'row'=4,'col'=4] {'row'}, use_global_device_ids=true, to_apply=%region_19.20.clone | all-reduce | flops 8192 | bytes 65536
  734.7 19.5 %all-reduce = f32[8192]{0:T(1024)S(1)} all-reduce(f32[8192]{0:T(1024)S(1)} %get-tuple-element.409), channel_id=2, replica_groups=mesh['groups'=2,'row'=4,'col'=4] {'col'}, use_global_device_ids=true, to_apply=%region_18.19.clone | all-reduce | flops 8192 | bytes 65536
  754.3 9.7 %reduce-scatter.5.cloned.1.call-done = f32[16,2048]{1,0:T(8,128)} async-done(((f32[16,8192]{1,0:T(8,128)}), f32[16,2048]{1,0:T(8,128)}) %reduce-scatter.5.cloned.1.call-update) | async-done | bytes 131088 | tf_op jit(solution)/shard_map/reduce_scatter | solution.py:66
  765.3 60.8 %all-reduce.2 = (f32[16,16]{1,0:T(8,128)S(1)}, f32[16,16]{1,0:T(8,128)S(1)}) all-reduce(f32[16,16]{1,0:T(8,128)S(1)} %fusion.77, f32[16,16]{1,0:T(8,128)S(1)} %convolution_bitcast_fusion), channel_id=1, replica_groups=mesh['groups'=2,'row'=4,'col'=4] {'row','col'}, use_global_device_ids=true, to_apply=%region_25.27 | all-reduce | flops 512 | bytes 4096 | tf_op jit(solution)/shard_map/psum | solution.py:147
  831.3 30.5 %psum.23 = f32[16,16]{1,0:T(8,128)S(1)} all-reduce(f32[16,16]{1,0:T(8,128)S(1)} %fusion.78), channel_id=1, replica_groups=mesh['groups'=2,'row'=4,'col'=4] {'row','col'}, use_global_device_ids=true, to_apply=%region_26.30 | all-reduce | flops 256 | bytes 2048 | tf_op jit(solution)/shard_map/psum | solution.py:154
  (402 shorter events, 249.4 us)
Async XLA Ops:
  7.2 35.2 %all-gather.3.cloned.1.call-start = ((), (), s32[]{:S(2)}) async-start(), calls=%async_computation.2 | async-start | bytes 1310720 | tf_op jit(solution)/shard_map/all_gather | solution.py:80
  7.9 0.9 copy-start
  7.9 52.2 %all-gather.5.cloned.1.call-start = ((), (), s32[]{:S(2)}) async-start(), calls=%async_computation.3 | async-start | bytes 1310720 | tf_op jit(solution)/shard_map/all_gather | solution.py:84
  8.7 745.7 %reduce-scatter.3.cloned.1.call-start = ((), (), s32[]{:S(2)}) async-start(), calls=%async_computation.4 | async-start | bytes 655360 | tf_op jit(solution)/shard_map/reduce_scatter | solution.py:59
  42.4 17.9 %copy-start.4 = (f32[32,8192]{1,0:T(8,128)S(1)}, f32[32,8192]{1,0:T(8,128)}, u32[]{:S(2)}) copy-start(f32[32,8192]{1,0:T(8,128)} %all-gather.3.cloned.1.call-done) | copy-start | bytes 3145732
  60.2 0.7 copy-start.8
  60.2 0.7 copy-start.9
  719.0 0.8 copy-start.2
  719.0 1.0 copy-start.1
  719.8 44.2 %reduce-scatter.5.cloned.1.call-start = ((), (), s32[]{:S(2)}) async-start(), calls=%async_computation.5 | async-start | bytes 655360 | tf_op jit(solution)/shard_map/reduce_scatter | solution.py:66
  719.9 3.7 copy-start.5
  720.4 0.7 copy-start.13
  721.1 0.7 copy-start.12
  734.7 19.6 %copy-start.11 = (f32[2048]{0:T(1024)S(1)}, f32[2048]{0:T(1024)}, u32[]{:S(2)}) copy-start(f32[2048]{0:T(1024)} %param.16) | copy-start | bytes 24580
  764.0 66.7 %copy-start.7 = (f32[16,2048]{1,0:T(8,128)S(1)}, f32[16,2048]{1,0:T(8,128)}, u32[]{:S(2)}) copy-start(f32[16,2048]{1,0:T(8,128)} %reduce-scatter.5.cloned.1.call-done) | copy-start | bytes 393220
  765.3 65.5 %copy-start.6 = (f32[16,2048]{1,0:T(8,128)S(1)}, f32[16,2048]{1,0:T(8,128)}, u32[]{:S(2)}) copy-start(f32[16,2048]{1,0:T(8,128)} %reduce-scatter.3.cloned.1.call-done) | copy-start | bytes 393220
  831.1 35.2 %copy-start.3 = (f32[16,2048]{1,0:T(8,128)}, f32[16,2048]{1,0:T(8,128)S(1)}, u32[]{:S(2)}) copy-start(f32[16,2048]{1,0:T(8,128)S(1)} %convolution_subtract_fusion) | copy-start | bytes 393220
  866.3 1.0 copy-start.10
Sparse Core Ops, SparseCore 0:
  9.6 32.7 all-gather.2
  44.0 16.1 all-gather.4
  719.9 21.7 reduce-scatter.2
  744.1 19.8 reduce-scatter.4
where the time goes:
time: 883 us; the launch traced here: 875 us
  loops' own time  326 us (37%)
  matrix products  276 us (31%)
  blocking collectives  149 us (17%)
  other arithmetic  46.4 us (5%)
  waiting for transfers between devices  35.3 us (4%)
  local copies, waits for them, and re-layouts  25.9 us (3%)
  between operations  15.3 us (2%)
    another operation x1, loops' own time, on_device(): carried = lax.fori_loop(0, row_slots.shape[0] // 4, one_turn, initial)  326 us
    dot_general x64, matrix products, tile_kernel(): lax.dot_general(row_points, col_points, (((0,), (0,)), ((), ())), precisi...  170 us
    dot_general x64, matrix products, one_tile(): lax.dot_general(dir_cols, kernel, (((1,), (1,)), ((), ())), precision=HIG...  61.8 us
    psum x1, blocking collectives, on_device(): lax.psum((gram(direction, image), gram(residual, residual)), ('row', 'col'))  60.8 us
    dot_general x64, matrix products, one_tile(): lax.dot_general(dir_rows, kernel, (((1,), (0,)), ((), ())), precision=HIG...  39.9 us
    psum x1, blocking collectives, on_device(): lax.psum(gram(residual_next, residual_next), ('row', 'col'))  30.5 us
    unnamed x2, blocking collectives  30.4 us
    dynamic_update_slice x128, other arithmetic, add_at(): lax.dynamic_update_slice_in_dim(running, current + addend, start, axis_last)  21.8 us
  transfers between devices with their start and end apart: 4, of which 3 were waited for; matrix products, arithmetic and copies ran while one was open for 0% of the time, Pallas kernels for 0%

commit v1 on v0

--- a/solution.py
+++ b/solution.py
@@ -6,6 +6,27 @@
 
 BLK_DEV = 4
 HIGH = lax.Precision.HIGHEST
+
+
+def in_order(parts, dim):
+    parts = jnp.moveaxis(parts, 0, dim)
+    dims = parts.shape
+    return parts.reshape(*dims[:dim], dims[dim] * dims[dim + 1], *dims[dim + 2 :])
+
+
+def grow_blocks(x, axis):
+    length, position = (lax.axis_size(axis), lax.axis_index(axis))
+    pieces, bit = (x[None], 1)
+    while bit < length:
+        theirs = lax.ppermute(pieces, axis, [(i, i ^ bit) for i in range(length)])
+        low = position & bit == 0
+        pieces = jnp.concatenate([jnp.where(low, pieces, theirs), jnp.where(low, theirs, pieces)])
+        bit *= 2
+    return pieces
+
+
+def doubled_up(shard, axis, dim):
+    return in_order(grow_blocks(shard, axis), dim)
 
 
 def tile_kernel(row_points, col_points):
@@ -81,7 +102,7 @@
         lax.all_gather(direction, "col", axis=1, tiled=True),
     )
     col_feat, col_dir = (
-        lax.all_gather(features, "row", axis=1, tiled=True),
+        doubled_up(features, "row", 1),
         lax.all_gather(direction, "row", axis=1, tiled=True),
     )
     side_count = direction.shape[0]

time: 883 us -> 867 us (0.982)
  waiting for transfers between devices: 35.3 us -> 16 us
    all_gather x1 -> x0, waiting for transfers between devices: 17.7 us -> none  [on_device(): lax.all_gather(features, 'row', axis=1, tiled=True)]
  transfers between devices with their start and end apart: 4 -> 5, of which waited for: 3 -> 3; matrix products, arithmetic and copies ran while one was open for 0% -> 0% of each run, Pallas kernels for 0% -> 0%
where the time goes in v1:
time: 867 us; the launch traced here: 858 us
  loops' own time  326 us (38%)
  matrix products  276 us (32%)
  blocking collectives  148 us (17%)
  other arithmetic  46.6 us (5%)
  local copies, waits for them, and re-layouts  25.9 us (3%)
  waiting for transfers between devices  16 us (2%)
  between operations  15.3 us (2%)
    another operation x1, loops' own time, on_device(): carried = lax.fori_loop(0, row_slots.shape[0] // 4, one_turn, initial)  326 us
    dot_general x64, matrix products, tile_kernel(): lax.dot_general(row_points, col_points, (((0,), (0,)), ((), ())), precisi...  170 us
    dot_general x64, matrix products, one_tile(): lax.dot_general(dir_cols, kernel, (((1,), (1,)), ((), ())), precision=HIG...  61.8 us
    psum x1, blocking collectives, on_device(): lax.psum((gram(direction, image), gram(residual, residual)), ('row', 'col'))  60.8 us
    dot_general x64, matrix products, one_tile(): lax.dot_general(dir_rows, kernel, (((1,), (0,)), ((), ())), precision=HIG...  39.9 us
    psum x1, blocking collectives, on_device(): lax.psum(gram(residual_next, residual_next), ('row', 'col'))  30.5 us
    unnamed x2, blocking collectives  29.6 us
    dynamic_update_slice x128, other arithmetic, add_at(): lax.dynamic_update_slice_in_dim(running, current + addend, start, axis_last)  21.8 us
  transfers between devices with their start and end apart: 5, of which 3 were waited for; matrix products, arithmetic and copies ran while one was open for 0% of the time, Pallas kernels for 0%

profile of v1, /device:TPU:0, one launch (start us, length us, event | category | flops | bytes accessed | tf_op | source)
XLA Modules:
  0.0 857.9 jit_solution(7014350370492927009)
XLA Ops:
  9.2 2.9 collective-permute-start.1
  12.1 20.8 %all_gather.11 = f32[16,8192]{1,0:T(8,128)S(1)} all-gather(f32[16,2048]{1,0:T(8,128)S(1)} %copy-done), channel_id=1, replica_groups=mesh['groups'=2,'row'=4,'col'=4] {'col'}, dimensions={1}, use_global_device_ids=true | all-gather | bytes 655360 | tf_op jit(solution)/shard_map/all_gather | solution.py:102
  32.9 6.5 all_gather.9
  39.6 4.2 all-gather.2.cloned.1.call-done
  44.5 657.9 %while.22 = (s32[]{:T(128)}, f32[16,8192]{1,0:T(8,128)S(1)}, f32[8192]{0:T(1024)S(1)}, f32[16,8192]{1,0:T(8,128)S(1)}, f32[8192]{0:T(1024)S(1)}, /*index=5*/s32[...) while((s32[]{:T(128)}, f32[16,8192]{1,0:T(8,128)S(1)}, ...), condition=%wide.region_17.18_spmd, body=%wide.region_0.17_spmd.sunk | while | flops 821393472 | bytes 14518369 | solution.py:163
  67.3 2.7 fusion.148
  71.9 2.7 fusion.150
  108.4 2.7 fusion.148
  113.0 2.7 fusion.150
  117.6 2.7 fusion.152
  149.6 2.6 fusion.148
  154.2 2.7 fusion.150
  158.8 2.6 fusion.152
  190.7 2.7 fusion.148
  195.3 2.7 fusion.150
  199.9 2.6 fusion.152
  231.8 2.7 fusion.148
  236.4 2.7 fusion.150
  272.9 2.7 fusion.148
  277.5 2.7 fusion.150
  314.0 2.7 fusion.148
  318.6 2.7 fusion.150
  355.1 2.7 fusion.148
  359.7 2.7 fusion.150
  364.3 2.7 fusion.152
  396.3 2.7 fusion.148
  400.9 2.7 fusion.150
  437.4 2.7 fusion.148
  442.0 2.7 fusion.150
  478.5 2.7 fusion.148
  483.1 2.7 fusion.150
  519.6 2.7 fusion.148
  524.2 2.7 fusion.150
  560.7 2.7 fusion.148
  565.3 2.7 fusion.150
  569.9 2.7 fusion.152
  601.8 2.7 fusion.148
  606.4 2.7 fusion.150
  642.9 2.7 fusion.148
  647.5 2.7 fusion.150
  684.0 2.7 fusion.148
  688.6 2.7 fusion.150
  697.8 2.7 fusion.154
  707.5 12.1 %all-reduce.1 = f32[8192]{0:T(1024)S(1)} all-reduce(f32[8192]{0:T(1024)S(1)} %get-tuple-element.410), channel_id=3, replica_groups=mesh['groups'=2,'row'=4,'col'=4] {'row'}, use_global_device_ids=true, to_apply=%region_19.20.clone | all-reduce | flops 8192 | bytes 65536
  719.6 17.5 %all-reduce = f32[8192]{0:T(1024)S(1)} all-reduce(f32[8192]{0:T(1024)S(1)} %get-tuple-element.409), channel_id=2, replica_groups=mesh['groups'=2,'row'=4,'col'=4] {'col'}, use_global_device_ids=true, to_apply=%region_18.19.clone | all-reduce | flops 8192 | bytes 65536
  737.1 9.9 %reduce-scatter.5.cloned.1.call-done = f32[16,2048]{1,0:T(8,128)} async-done(((f32[16,8192]{1,0:T(8,128)}), f32[16,2048]{1,0:T(8,128)}) %reduce-scatter.5.cloned.1.call-update) | async-done | bytes 131088 | tf_op jit(solution)/shard_map/reduce_scatter | solution.py:87
  748.3 60.8 %all-reduce.2 = (f32[16,16]{1,0:T(8,128)S(1)}, f32[16,16]{1,0:T(8,128)S(1)}) all-reduce(f32[16,16]{1,0:T(8,128)S(1)} %fusion.77, f32[16,16]{1,0:T(8,128)S(1)} %convolution_bitcast_fusion), channel_id=1, replica_groups=mesh['groups'=2,'row'=4,'col'=4] {'row','col'}, use_global_device_ids=true, to_apply=%region_25.27 | all-reduce | flops 512 | bytes 4096 | tf_op jit(solution)/shard_map/psum | solution.py:168
  814.4 30.5 %psum.23 = f32[16,16]{1,0:T(8,128)S(1)} all-reduce(f32[16,16]{1,0:T(8,128)S(1)} %fusion.78), channel_id=1, replica_groups=mesh['groups'=2,'row'=4,'col'=4] {'row','col'}, use_global_device_ids=true, to_apply=%region_26.30 | all-reduce | flops 256 | bytes 2048 | tf_op jit(solution)/shard_map/psum | solution.py:175
  (408 shorter events, 250.1 us)
Async XLA Ops:
  7.2 1.9 copy-start.5
  7.2 36.7 %all-gather.2.cloned.1.call-start = ((), (), s32[]{:S(2)}) async-start(), calls=%async_computation.2 | async-start | bytes 1310720 | tf_op jit(solution)/shard_map/all_gather | solution.py:101
  7.2 1.9 collective-permute-start
  7.9 729.2 %reduce-scatter.3.cloned.1.call-start = ((), (), s32[]{:S(2)}) async-start(), calls=%async_computation.3 | async-start | bytes 655360 | tf_op jit(solution)/shard_map/reduce_scatter | solution.py:80
  9.2 3.0 copy-start
  9.2 30.2 %collective-permute-start.1 = (f32[2,32,2048]{2,1,0:T(8,128)S(1)}, f32[2,32,2048]{2,1,0:T(8,128)S(1)}, u32[]{:S(2)}, u32[]{:S(2)}) collective-permute-start(f32[2,32,2048]{2,1,0:T(8,128)S(1)} %pad_maximum_fusion), channel_id=1, source_target_pairs={{0,8},{4,12},{8,0},{12,4},{1,9},{5,13},{9,1},{13,5},{2,10},{6,14},... | collective-permute-start | bytes 1572872 | tf_op jit(solution)/shard_map/ppermute | solution.py:21
  43.9 0.7 copy-start.8
  43.9 0.7 copy-start.9
  702.4 0.8 copy-start.2
  702.5 1.0 copy-start.1
  703.3 43.8 %reduce-scatter.5.cloned.1.call-start = ((), (), s32[]{:S(2)}) async-start(), calls=%async_computation.4 | async-start | bytes 655360 | tf_op jit(solution)/shard_map/reduce_scatter | solution.py:87
  703.3 3.9 copy-start.4
  704.0 0.7 copy-start.13
  704.7 0.7 copy-start.12
  719.6 17.5 %copy-start.11 = (f32[2048]{0:T(1024)S(1)}, f32[2048]{0:T(1024)}, u32[]{:S(2)}) copy-start(f32[2048]{0:T(1024)} %param.16) | copy-start | bytes 24580
  747.1 66.7 %copy-start.7 = (f32[16,2048]{1,0:T(8,128)S(1)}, f32[16,2048]{1,0:T(8,128)}, u32[]{:S(2)}) copy-start(f32[16,2048]{1,0:T(8,128)} %reduce-scatter.5.cloned.1.call-done) | copy-start | bytes 393220
  748.3 65.5 %copy-start.6 = (f32[16,2048]{1,0:T(8,128)S(1)}, f32[16,2048]{1,0:T(8,128)}, u32[]{:S(2)}) copy-start(f32[16,2048]{1,0:T(8,128)} %reduce-scatter.3.cloned.1.call-done) | copy-start | bytes 393220
  814.2 35.2 %copy-start.3 = (f32[16,2048]{1,0:T(8,128)}, f32[16,2048]{1,0:T(8,128)S(1)}, u32[]{:S(2)}) copy-start(f32[16,2048]{1,0:T(8,128)S(1)} %convolution_subtract_fusion) | copy-start | bytes 393220
  849.4 1.0 copy-start.10
Sparse Core Ops, SparseCore 0:
  9.6 34.2 all-gather.1
  703.4 21.1 reduce-scatter.2
  727.0 19.9 reduce-scatter.4
